TPU v7x, 32 devices: a whole 2x2x4 slice. The times are simulated.
32 devices in a mesh: leaf: 16 (over z, y, x), cone: 2 (over core).
Axes of the slice: x: 2, y: 2, z: 4, core: 2. Of those that a mesh axis runs over, the one named last changes fastest.
Arguments:
- coefficients: bfloat16 [128, 4, 3, 32, 256], P('leaf', 'cone'), may hold values from -6 to 6
- local_to_target: bfloat16 [128, 4, 256, 768], P('leaf', 'cone'), may hold values from -0.1875 to 0.1875
- send_map: int32 [16, 16, 32], P('leaf'), may hold values from -1 to 255, as said below
- test_weight: bfloat16 [16, 16, 32, 108], P('leaf'), may hold values from -1 to 1
- slot_edge: int32 [3, 16, 16, 32], P(None, 'leaf'), may hold values from -1 to 383, as said below
- shared_edges: int32 [16, 2, 32], P('leaf'), may hold values from 0 to 383, as said below
Outputs:
- tested: float32 [2, 32, 6144], P(None, 'cone', 'leaf')
Inputs may be any that keep to these rules, and one draw needn't show every extreme that they name: Each of the 256 triangles of a leaf device s stands in exactly one slot of send_map[s]; every other slot is -1. In every draw, each leaf device fills all 32 slots of its block to some owner. slot_edge[e, d, s, n] is -1 exactly where send_map[s, d, n] is -1. The 64 numbers of shared_edges[d] are distinct.
All inputs are finite; a program needn't handle non-finite values.
Results may differ from a plain program's by a relative error of at most 0.0029.
Values may be sent and summed in bfloat16 or wider, within the bound.
A program may use at most 64 MiB of HBM per device.

v0:
```python
import jax
import jax.numpy as jnp
from jax import lax
from jax.sharding import PartitionSpec as P

QUAD = 12
TRI_LEAF = 32
EDGE_DEV = 384


def extended(array, sides, width):
    for axis, dim in sides:
        peers, length = (lax.axis_size(axis), array.shape[dim])
        up = [(i, (i + 1) % peers) for i in range(peers - 1)]
        down = [(j, i) for i, j in up]
        last = lax.slice_in_dim(array, length - width, length, axis=dim)
        leading = lax.slice_in_dim(array, 0, width, axis=dim)
        before = lax.ppermute(last, axis, up)
        after = lax.ppermute(leading, axis, down)
        array = jnp.concatenate([before, array, after], axis=dim)
    return array


def tested_slots(weights, fields, rhs_count, result_form):
    peer_count, capacity = (weights.shape[0], weights.shape[1])
    weight_view = weights.reshape(peer_count, capacity, 3, QUAD, 3)
    field_view = fields.reshape(peer_count, capacity, QUAD, 2, 3, rhs_count)
    return jnp.einsum(
        "scepk,scpikh->" + result_form, weight_view, field_view, preferred_element_type=jnp.float32
    )


def body(coefficients, local_to_target, send_map, test_weight, slot_edge, shared_edges):
    partial_field = jnp.einsum(
        "lkchr,lkrq->lqch", coefficients, local_to_target, preferred_element_type=jnp.float32
    )
    cone_count = lax.axis_size("cone")
    rhs_count = partial_field.shape[3] // cone_count
    summed = lax.psum(partial_field, "cone")
    rhs_share = lax.dynamic_slice_in_dim(summed, lax.axis_index("cone") * rhs_count, rhs_count, 3)
    rhs_share = rhs_share.astype(jnp.bfloat16)
    leaf_count = rhs_share.shape[0]
    tri_rows = rhs_share.reshape(leaf_count * TRI_LEAF, -1)
    send_rows = send_map[0]
    is_live = send_rows >= 0
    safe_rows = jnp.where(is_live, send_rows, 0)
    picked = tri_rows[safe_rows]
    outgoing = jnp.where(is_live[:, :, None], picked, jnp.zeros((), jnp.bfloat16))
    weights = test_weight[0]
    arrived = lax.all_to_all(outgoing, "leaf", split_axis=0, concat_axis=0, tiled=True)
    partial_value = tested_slots(weights, arrived, rhs_count, "escih")
    edge_ids = slot_edge[:, 0].reshape(-1)
    values = partial_value.reshape(-1, 2 * rhs_count)
    onehot = (edge_ids[:, None] == jnp.arange(EDGE_DEV, dtype=jnp.int32)[None, :]).astype(
        jnp.float32
    )
    edge_sum = jnp.einsum(
        "ra,re->ae",
        values,
        onehot,
        precision=lax.Precision.HIGHEST,
        preferred_element_type=jnp.float32,
    )
    lower_ids = shared_edges[0, 0]
    upper_ids = shared_edges[0, 1]
    share_width = lower_ids.shape[0]
    rim_values = jnp.concatenate([edge_sum[:, lower_ids], edge_sum[:, upper_ids]], axis=1)
    padded = extended(rim_values, (("leaf", 1),), share_width)
    total = (
        edge_sum.at[:, lower_ids]
        .add(padded[:, :share_width])
        .at[:, upper_ids]
        .add(padded[:, 3 * share_width :])
    )
    return total.reshape(2, rhs_count, -1)


def solution(mesh):
    placed = (
        P("leaf", "cone", None, None, None),
        P("leaf", "cone", None, None),
        P("leaf", None, None),
        P("leaf", None, None, None),
        P(None, "leaf", None, None),
        P("leaf", None, None),
    )
    return jax.shard_map(
        body, mesh=mesh, in_specs=placed, out_specs=P(None, "cone", "leaf"), check_vma=False
    )
```

profile of v0, /device:TPU:6, one launch (start us, length us, event | category | flops | bytes accessed | tf_op | source)
XLA Modules:
  0.0 120.5 jit_solution(16568541062340450514)
XLA Ops:
  0.0 0.8 compare_select_fusion
  0.8 0.7 compare_bitcast_fusion
  1.5 5.3 %fusion.3 = f32[8,768,3,32]{1,3,2,0:T(8,128)} fusion(bf16[8,2,3,32,256]{4,3,2,1,0:T(8,128)(2,1)S(1)} %copy-done, bf16[8,2,256,768]{3,2,1,0:T(8,128)(2,1)} %param.7), kind=kOutput, calls=%fused_computation.9 | convolution fusion | flops 603979776 | bytes 9437184 | tf_op jit(solution)/shard_map/lkchr,lkrq->lqch/dot_general | solution.py:34
  6.8 10.3 %all-reduce.1 = bf16[8,768,3,32]{1,3,2,0:T(8,128)(2,1)S(1)} all-reduce(f32[8,768,3,32]{1,3,2,0:T(8,128)} %fusion.3), channel_id=1, replica_groups=mesh['leaf'=16,'cone'=2] {'cone'}, use_global_device_ids=true, to_apply=%region_0.0 | all-reduce | flops 589824 | bytes 3538944 | tf_op jit(solution)/shard_map/psum | solution.py:39
  17.1 6.7 %copy.25 = bf16[8,768,3,16]{3,2,1,0:T(4,128)(2,1)} copy(bf16[8,768,3,16]{1,3,2,0:T(8,128)(2,1)S(1)} %dynamic-slice_convert_fusion) | data formatting | bytes 1179648 | tf_op jit(solution)/shard_map/convert_element_type | solution.py:41
  23.9 9.3 %reshape.102 = bf16[256,1152]{1,0:T(8,128)(2,1)S(1)} reshape(bf16[8,768,3,16]{3,2,1,0:T(4,128)(2,1)} %copy.25) | data formatting | bytes 1179648 | tf_op jit(solution)/shard_map/reshape | solution.py:43
  33.3 2.1 %gather_fusion = bf16[512,1152]{1,0:T(8,128)(2,1)S(1)} fusion(bf16[256,1152]{1,0:T(8,128)(2,1)S(1)} %reshape.102, s32[1024]{0:T(1024)S(1)} %pad_clamp_fusion.2), kind=kCustom, calls=%fused_computation | custom fusion | bytes 2361344 | tf_op jit(solution)/shard_map/gather | solution.py:47
  35.4 1.2 %broadcast_select_fusion = bf16[16,32,1152]{2,1,0:T(8,128)(2,1)} fusion(bf16[16,32,1152]{2,1,0:T(8,128)(2,1)S(1)} %bitcast.58, pred[16,32]{1,0:T(8,128)(4,1)S(1)} %compare_bitcast_fusion), kind=kLoop, calls=%fused_computation.13 | loop fusion | flops 589824 | bytes 2359808 | tf_op jit(solution)/shard_map/jit(_where)/select_n | solution.py:48
  36.6 7.4 %all-to-all-start = ((bf16[16,32,1152]{2,1,0:T(8,128)(2,1)}), bf16[16,32,1152]{2,1,0:T(8,128)(2,1)S(1)}, u32[]{:S(2)}, u32[]{:S(2)}) async-start(bf16[16,32,1152]{2,1,0:T(8,128)(2,1)} %broadcast_select_fusion), calls=%async_computation | async-start | bytes 2359296 | tf_op jit(solution)/shard_map/all_to_all | solution.py:50
  44.4 2.5 %copy.37 = bf16[16,32,3,12,3,1]{3,2,4,5,1,0:T(4,128)(2,1)} copy(bf16[16,32,3,12,3,1]{1,0,4,3,2,5:T(8,128)(2,1)S(1)} %bitcast.59) | data formatting | bytes 221184 | tf_op jit(solution)/shard_map/reshape;squeeze | solution.py:26
  47.1 23.8 %all-to-all-done = bf16[16,32,1152]{2,1,0:T(8,128)(2,1)S(1)} async-done(((bf16[16,32,1152]{2,1,0:T(8,128)(2,1)}), bf16[16,32,1152]{2,1,0:T(8,128)(2,1)S(1)}, u32[]{:S(2)}, u32[]{:S(2)}) %all-to-all-start) | async-done | bytes 1179680 | tf_op jit(solution)/shard_map/all_to_all | solution.py:50
  70.9 3.3 %copy.26 = bf16[16,32,1152]{1,2,0:T(8,128)(2,1)} copy(bf16[16,32,1152]{2,1,0:T(8,128)(2,1)S(1)} %all-to-all-done) | data formatting | bytes 2359296 | tf_op jit(solution)/shard_map/all_to_all | solution.py:50
  74.2 19.7 %copy.28 = bf16[16,32,12,2,3,16]{5,2,4,3,1,0:T(8,128)(2,1)} copy(bf16[16,32,12,2,3,16]{1,5,4,3,2,0:T(8,128)(2,1)} %bitcast.57) | data formatting | bytes 2359296 | tf_op jit(solution)/shard_map/reshape | solution.py:27
  93.9 6.6 %convolution_bitcast_fusion = f32[3,16,32,2,16]{4,0,3,2,1:T(4,128)} fusion(bf16[16,32,12,2,3,16]{5,2,4,3,1,0:T(8,128)(2,1)} %copy.28, bf16[16,32,3,12,3,1]{3,2,4,5,1,0:T(4,128)(2,1)S(1)} %copy-done.1), kind=kOutput, calls=%fused_computation.10 | convolution fusion | flops 3538944 | bytes 1486848 | tf_op jit(solution)/shard_map/scepk,scpikh->escih/dot_general | solution.py:28
  100.5 1.8 %copy.30 = f32[3,16,32,2,16]{2,1,0,4,3:T(8,128)S(1)} copy(f32[3,16,32,2,16]{4,0,3,2,1:T(4,128)} %convolution_bitcast_fusion) | data formatting | bytes 393216 | tf_op jit(solution)/shard_map/scepk,scpikh->escih/transpose | solution.py:28
  102.7 2.2 %fusion.2 = f32[32,384]{0,1:T(8,128)S(1)} fusion(f32[1536,32]{0,1:T(8,128)S(1)} %reshape.104, s32[1536]{0:T(1024)S(1)} %eq.15), kind=kOutput, calls=%fused_computation.8 | convolution fusion | flops 227082240 | bytes 251904 | tf_op jit(solution)/shard_map/ra,re->ae/dot_general | solution.py:57
  104.9 0.6 gather_fusion.1
  105.5 5.4 %collective-permute-start = (f32[32,32]{0,1:T(8,128)S(1)}, f32[32,32]{0,1:T(8,128)S(1)}, u32[]{:S(2)}, u32[]{:S(2)}) collective-permute-start(f32[32,32]{0,1:T(8,128)S(1)} %bitcast.61), channel_id=1, source_target_pairs={{0,2},{2,4},{4,6},{6,8},{8,10},{10,12},{12,14},{14,16},{16,18},{18... | collective-permute-start | bytes 12296 | tf_op jit(solution)/shard_map/ppermute | solution.py:18
  111.0 0.6 gather_fusion.2
  111.5 1.9 %collective-permute-start.1 = (f32[32,32]{0,1:T(8,128)S(1)}, f32[32,32]{0,1:T(8,128)S(1)}, u32[]{:S(2)}, u32[]{:S(2)}) collective-permute-start(f32[32,32]{0,1:T(8,128)S(1)} %bitcast.60), channel_id=1, source_target_pairs={{2,0},{4,2},{6,4},{8,6},{10,8},{12,10},{14,12},{16,14},{18,16},{20... | collective-permute-start | bytes 12296 | tf_op jit(solution)/shard_map/ppermute | solution.py:19
  113.5 0.8 scatter_custom_fusion
  114.3 4.6 %collective-permute-done.1 = f32[32,32]{0,1:T(8,128)S(1)} collective-permute-done((f32[32,32]{0,1:T(8,128)S(1)}, f32[32,32]{0,1:T(8,128)S(1)}, u32[]{:S(2)}, u32[]{:S(2)}) %collective-permute-start.1) | collective-permute-done | bytes 4128 | tf_op jit(solution)/shard_map/ppermute | solution.py:19
  119.0 0.8 scatter_custom_fusion.1
  119.8 0.7 copy.34
  (19 shorter events, 1.0 us)
Async XLA Ops:
  0.0 1.5 %copy-start = (bf16[8,2,3,32,256]{4,3,2,1,0:T(8,128)(2,1)S(1)}, bf16[8,2,3,32,256]{4,3,2,1,0:T(8,128)(2,1)}, u32[]{:S(2)}) copy-start(bf16[8,2,3,32,256]{4,3,2,1,0:T(8,128)(2,1)} %param.6) | copy-start | bytes 2359300
  35.4 8.6 %copy-start.2 = (bf16[1,16,32,108]{3,2,1,0:T(8,128)(2,1)S(1)}, bf16[1,16,32,108]{3,2,1,0:T(8,128)(2,1)}, u32[]{:S(2)}) copy-start(bf16[1,16,32,108]{3,2,1,0:T(8,128)(2,1)} %param.9) | copy-start | bytes 331780
  36.6 10.3 %copy-start.3 = (s32[3,1,16,32]{3,2,1,0:T(8,128)S(1)}, s32[3,1,16,32]{3,2,1,0:T(8,128)}, u32[]{:S(2)}) copy-start(s32[3,1,16,32]{3,2,1,0:T(8,128)} %param.10) | copy-start | bytes 18436
  36.6 10.4 %copy-start.4 = (s32[1,2,32]{2,1,0:T(2,128)S(1)}, s32[1,2,32]{2,1,0:T(2,128)}, u32[]{:S(2)}) copy-start(s32[1,2,32]{2,1,0:T(2,128)} %param.11) | copy-start | bytes 772
  36.6 34.2 %all-to-all-start = ((bf16[16,32,1152]{2,1,0:T(8,128)(2,1)}), bf16[16,32,1152]{2,1,0:T(8,128)(2,1)S(1)}, u32[]{:S(2)}, u32[]{:S(2)}) async-start(bf16[16,32,1152]{2,1,0:T(8,128)(2,1)} %broadcast_select_fusion), calls=%async_computation | async-start | bytes 2359296 | tf_op jit(solution)/shard_map/all_to_all | solution.py:50
  74.2 19.7 %copy-start.1 = (bf16[16,32,3,12,3,1]{3,2,4,5,1,0:T(4,128)(2,1)S(1)}, bf16[16,32,3,12,3,1]{3,2,4,5,1,0:T(4,128)(2,1)}, u32[]{:S(2)}) copy-start(bf16[16,32,3,12,3,1]{3,2,4,5,1,0:T(4,128)(2,1)} %copy.37) | copy-start | bytes 331780
  105.5 7.9 %collective-permute-start = (f32[32,32]{0,1:T(8,128)S(1)}, f32[32,32]{0,1:T(8,128)S(1)}, u32[]{:S(2)}, u32[]{:S(2)}) collective-permute-start(f32[32,32]{0,1:T(8,128)S(1)} %bitcast.61), channel_id=1, source_target_pairs={{0,2},{2,4},{4,6},{6,8},{8,10},{10,12},{12,14},{14,16},{16,18},{18... | collective-permute-start | bytes 12296 | tf_op jit(solution)/shard_map/ppermute | solution.py:18
  111.5 7.4 %collective-permute-start.1 = (f32[32,32]{0,1:T(8,128)S(1)}, f32[32,32]{0,1:T(8,128)S(1)}, u32[]{:S(2)}, u32[]{:S(2)}) collective-permute-start(f32[32,32]{0,1:T(8,128)S(1)} %bitcast.60), channel_id=1, source_target_pairs={{2,0},{4,2},{6,4},{8,6},{10,8},{12,10},{14,12},{16,14},{18,16},{20... | collective-permute-start | bytes 12296 | tf_op jit(solution)/shard_map/ppermute | solution.py:19
where the time goes:
time: 121 us
  local copies, waits for them, and re-layouts  48.4 us (40%)
  waiting for transfers between devices  28.4 us (23%)
  starting transfers between devices  14.7 us (12%)
  matrix products  14.2 us (12%)
  blocking collectives  10.3 us (9%)
  other arithmetic  4.39 us (4%)
    all_to_all x1, waiting for transfers between devices, body(): lax.all_to_all(outgoing, 'leaf', split_axis=0, concat_axis=0, tiled=True)  23.8 us
    reshape x1, local copies, waits for them, and re-layouts, tested_slots(): field_view = fields.reshape(peer_count, capacity, QUAD, 2, 3, rhs_count)  19.7 us
    psum x1, blocking collectives, body(): summed = lax.psum(partial_field, 'cone')  10.3 us
    reshape x1, local copies, waits for them, and re-layouts, body(): tri_rows = rhs_share.reshape(leaf_count * TRI_LEAF, -1)  9.31 us
    all_to_all x1, starting transfers between devices, body(): lax.all_to_all(outgoing, 'leaf', split_axis=0, concat_axis=0, tiled=True)  7.4 us
    convert_element_type x2, local copies, waits for them, and re-layouts, body(): rhs_share = rhs_share.astype(jnp.bfloat16)  6.78 us
    dot_general x1, matrix products, tested_slots(): jnp.einsum('scepk,scpikh->' + result_form, weight_view, field_view, prefe...  6.63 us
    ppermute x1, starting transfers between devices, extended(): before = lax.ppermute(last, axis, up)  5.42 us
  transfers between devices with their start and end apart: 3, of which 2 were waited for; matrix products, arithmetic and copies ran while one was open for 4% of the time, Pallas kernels for 0%

commit v1 on v0

--- a/solution.py
+++ b/solution.py
@@ -6,6 +6,18 @@
 QUAD = 12
 TRI_LEAF = 32
 EDGE_DEV = 384
+
+
+def in_blocks(x, dim, size):
+    shape = x.shape
+    pieces = x.reshape(*shape[:dim], size, shape[dim] // size, *shape[dim + 1 :])
+    return jnp.moveaxis(pieces, dim, 0)
+
+
+def laid_out(blocks, dim):
+    dims = list(blocks.shape[1:])
+    dims[dim] *= blocks.shape[0]
+    return jnp.moveaxis(blocks, 0, dim).reshape(dims)
 
 
 def extended(array, sides, width):
@@ -47,7 +59,14 @@
     picked = tri_rows[safe_rows]
     outgoing = jnp.where(is_live[:, :, None], picked, jnp.zeros((), jnp.bfloat16))
     weights = test_weight[0]
-    arrived = lax.all_to_all(outgoing, "leaf", split_axis=0, concat_axis=0, tiled=True)
+    devices, here = (lax.axis_size("leaf"), lax.axis_index("leaf"))
+    tiles = in_blocks(outgoing, 0, devices)
+    outs = [tiles[here]]
+    for step in range(1, devices):
+        sent = tiles[here ^ step]
+        outs.append(lax.ppermute(sent, "leaf", [(i_2, i_2 ^ step) for i_2 in range(devices)]))
+    tiles = jnp.stack(outs)[here ^ jnp.arange(devices)]
+    arrived = laid_out(tiles, 0)
     partial_value = tested_slots(weights, arrived, rhs_count, "escih")
     edge_ids = slot_edge[:, 0].reshape(-1)
     values = partial_value.reshape(-1, 2 * rhs_count)

time: 121 us -> 133 us (1.099)
  waiting for transfers between devices: 28.4 us -> 7.32 us
  starting transfers between devices: 14.7 us -> 33.5 us
  local copies, waits for them, and re-layouts: 48.4 us -> 62.9 us
    ppermute x0 -> x15, starting transfers between devices: none -> 26.5 us  [body(): lax.ppermute(sent, 'leaf', [(i_2, i_2 ^ step) for i_2 in range(devices)])]
    all_to_all x1 -> x0, waiting for transfers between devices: 23.8 us -> none  [body(): lax.all_to_all(outgoing, 'leaf', split_axis=0, concat_axis=0, tiled=True)]
    another operation x0 -> x2, local copies, waits for them, and re-layouts: none -> 20.1 us  [the longest x1 19.5 us: tested_slots(): field_view = fields.reshape(peer_count, capacity, QUAD, 2, 3, rhs_count)]
    reshape x1 -> x0, local copies, waits for them, and re-layouts: 19.7 us -> none  [tested_slots(): field_view = fields.reshape(peer_count, capacity, QUAD, 2, 3, rhs_count)]
    unnamed x11 -> x32, local copies, waits for them, and re-layouts: 0.41 us -> 12.4 us
    all_to_all x1 -> x0, starting transfers between devices: 7.4 us -> none  [body(): lax.all_to_all(outgoing, 'leaf', split_axis=0, concat_axis=0, tiled=True)]
    gather x0 -> x2, local copies, waits for them, and re-layouts: none -> 5.34 us  [body(): tiles = jnp.stack(outs)[here ^ jnp.arange(devices)]]
    all_to_all x1 -> x0, local copies, waits for them, and re-layouts: 3.34 us -> none  [body(): lax.all_to_all(outgoing, 'leaf', split_axis=0, concat_axis=0, tiled=True)]
  transfers between devices with their start and end apart: 3 -> 17, of which waited for: 2 -> 2; matrix products, arithmetic and copies ran while one was open for 4% -> 11% of each run, Pallas kernels for 0% -> 0%
where the time goes in v1:
time: 133 us
  local copies, waits for them, and re-layouts  62.9 us (47%)
  starting transfers between devices  33.5 us (25%)
  matrix products  14.2 us (11%)
  blocking collectives  10.3 us (8%)
  waiting for transfers between devices  7.32 us (6%)
  other arithmetic  4.21 us (3%)
    ppermute x15, starting transfers between devices, body(): lax.ppermute(sent, 'leaf', [(i_2, i_2 ^ step) for i_2 in range(devices)])  26.5 us
    another operation x1, local copies, waits for them, and re-layouts, tested_slots(): field_view = fields.reshape(peer_count, capacity, QUAD, 2, 3, rhs_count)  19.5 us
    unnamed x32, local copies, waits for them, and re-layouts  12.4 us
    psum x1, blocking collectives, body(): summed = lax.psum(partial_field, 'cone')  10.3 us
    reshape x1, local copies, waits for them, and re-layouts, body(): tri_rows = rhs_share.reshape(leaf_count * TRI_LEAF, -1)  9.31 us
    convert_element_type x2, local copies, waits for them, and re-layouts, body(): rhs_share = rhs_share.astype(jnp.bfloat16)  6.76 us
    dot_general x1, matrix products, tested_slots(): jnp.einsum('scepk,scpikh->' + result_form, weight_view, field_view, prefe...  6.61 us
    gather x2, local copies, waits for them, and re-layouts, body(): tiles = jnp.stack(outs)[here ^ jnp.arange(devices)]  5.34 us
  transfers between devices with their start and end apart: 17, of which 2 were waited for; matrix products, arithmetic and copies ran while one was open for 11% of the time, Pallas kernels for 0%

profile of v1, /device:TPU:6, one launch (start us, length us, event | category | flops | bytes accessed | tf_op | source)
XLA Modules:
  0.0 132.7 jit_solution(3178544981450626007)
XLA Ops:
  1.5 5.3 %fusion.3 = f32[8,768,3,32]{1,3,2,0:T(8,128)} fusion(bf16[8,2,3,32,256]{4,3,2,1,0:T(8,128)(2,1)S(1)} %copy-done, bf16[8,2,256,768]{3,2,1,0:T(8,128)(2,1)} %param.7), kind=kOutput, calls=%fused_computation.10 | convolution fusion | flops 603979776 | bytes 9437184 | tf_op jit(solution)/shard_map/lkchr,lkrq->lqch/dot_general | solution.py:46
  6.8 10.3 %all-reduce.1 = bf16[8,768,3,32]{1,3,2,0:T(8,128)(2,1)S(1)} all-reduce(f32[8,768,3,32]{1,3,2,0:T(8,128)} %fusion.3), channel_id=1, replica_groups=mesh['leaf'=16,'cone'=2] {'cone'}, use_global_device_ids=true, to_apply=%region_0.0 | all-reduce | flops 589824 | bytes 3538944 | tf_op jit(solution)/shard_map/psum | solution.py:51
  17.1 6.7 %copy.24 = bf16[8,768,3,16]{3,2,1,0:T(4,128)(2,1)} copy(bf16[8,768,3,16]{1,3,2,0:T(8,128)(2,1)S(1)} %dynamic-slice_convert_fusion) | data formatting | bytes 1179648 | tf_op jit(solution)/shard_map/convert_element_type | solution.py:53
  23.9 9.3 %reshape.147 = bf16[256,1152]{1,0:T(8,128)(2,1)S(1)} reshape(bf16[8,768,3,16]{3,2,1,0:T(4,128)(2,1)} %copy.24) | data formatting | bytes 1179648 | tf_op jit(solution)/shard_map/reshape | solution.py:55
  33.3 2.1 %gather_fusion = bf16[512,1152]{1,0:T(8,128)(2,1)S(1)} fusion(bf16[256,1152]{1,0:T(8,128)(2,1)S(1)} %reshape.147, s32[1024]{0:T(1024)S(1)} %pad_clamp_fusion.3), kind=kCustom, calls=%fused_computation | custom fusion | bytes 2361344 | tf_op jit(solution)/shard_map/gather | solution.py:59
  38.2 2.9 %collective-permute-start.2 = (bf16[1,32,1152]{2,1,0:T(8,128)(2,1)}, bf16[1,32,1152]{2,1,0:T(8,128)(2,1)S(1)}, u32[]{:S(2)}, u32[]{:S(2)}) collective-permute-start(bf16[1,32,1152]{2,1,0:T(8,128)(2,1)} %get-tuple-element.17), channel_id=1, source_target_pairs={{0,6},{2,4},{4,2},{6,0},{8,14},{10,12},{12,10},{14,8},{16,22},{18,... | collective-permute-start | bytes 221192 | tf_op jit(solution)/shard_map/ppermute | solution.py:67
  45.1 1.6 %copy.50 = bf16[16,32,3,12,3,1]{3,2,4,5,1,0:T(4,128)(2,1)S(1)} copy(bf16[16,32,3,12,3,1]{1,0,4,3,2,5:T(8,128)(2,1)S(1)} %bitcast.122) | data formatting | bytes 221184 | tf_op jit(solution)/shard_map/reshape;squeeze | solution.py:38
  50.2 2.3 %collective-permute-start.6 = (bf16[1,32,1152]{2,1,0:T(8,128)(2,1)}, bf16[1,32,1152]{2,1,0:T(8,128)(2,1)S(1)}, u32[]{:S(2)}, u32[]{:S(2)}) collective-permute-start(bf16[1,32,1152]{2,1,0:T(8,128)(2,1)} %get-tuple-element.13), channel_id=1, source_target_pairs={{0,14},{2,12},{4,10},{6,8},{8,6},{10,4},{12,2},{14,0},{16,30},{18,... | collective-permute-start | bytes 221192 | tf_op jit(solution)/shard_map/ppermute | solution.py:67
  53.2 2.6 %collective-permute-start.7 = (bf16[1,32,1152]{2,1,0:T(8,128)(2,1)}, bf16[1,32,1152]{2,1,0:T(8,128)(2,1)S(1)}, u32[]{:S(2)}, u32[]{:S(2)}) collective-permute-start(bf16[1,32,1152]{2,1,0:T(8,128)(2,1)} %get-tuple-element.12), channel_id=1, source_target_pairs={{0,16},{2,18},{4,20},{6,22},{8,24},{10,26},{12,28},{14,30},{16,0},... | collective-permute-start | bytes 221192 | tf_op jit(solution)/shard_map/ppermute | solution.py:67
  57.3 2.5 %collective-permute-start.9 = (bf16[1,32,1152]{2,1,0:T(8,128)(2,1)}, bf16[1,32,1152]{2,1,0:T(8,128)(2,1)S(1)}, u32[]{:S(2)}, u32[]{:S(2)}) collective-permute-start(bf16[1,32,1152]{2,1,0:T(8,128)(2,1)} %get-tuple-element.10), channel_id=1, source_target_pairs={{0,20},{2,22},{4,16},{6,18},{8,28},{10,30},{12,24},{14,26},{16,4},... | collective-permute-start | bytes 221192 | tf_op jit(solution)/shard_map/ppermute | solution.py:67
  60.5 2.2 %collective-permute-start.10 = (bf16[1,32,1152]{2,1,0:T(8,128)(2,1)}, bf16[1,32,1152]{2,1,0:T(8,128)(2,1)S(1)}, u32[]{:S(2)}, u32[]{:S(2)}) collective-permute-start(bf16[1,32,1152]{2,1,0:T(8,128)(2,1)} %get-tuple-element.9), channel_id=1, source_target_pairs={{0,22},{2,20},{4,18},{6,16},{8,30},{10,28},{12,26},{14,24},{16,6},... | collective-permute-start | bytes 221192 | tf_op jit(solution)/shard_map/ppermute | solution.py:67
  63.4 3.6 %collective-permute-start.11 = (bf16[1,32,1152]{2,1,0:T(8,128)(2,1)}, bf16[1,32,1152]{2,1,0:T(8,128)(2,1)S(1)}, u32[]{:S(2)}, u32[]{:S(2)}) collective-permute-start(bf16[1,32,1152]{2,1,0:T(8,128)(2,1)} %get-tuple-element.8), channel_id=1, source_target_pairs={{0,24},{2,26},{4,28},{6,30},{8,16},{10,18},{12,20},{14,22},{16,8},... | collective-permute-start | bytes 221192 | tf_op jit(solution)/shard_map/ppermute | solution.py:67
  68.4 3.5 %collective-permute-start.13 = (bf16[1,32,1152]{2,1,0:T(8,128)(2,1)S(1)}, bf16[1,32,1152]{2,1,0:T(8,128)(2,1)S(1)}, u32[]{:S(2)}, u32[]{:S(2)}) collective-permute-start(bf16[1,32,1152]{2,1,0:T(8,128)(2,1)S(1)} %copy-done.3), channel_id=1, source_target_pairs={{0,28},{2,30},{4,24},{6,26},{8,20},{10,22},{12,16},{14,18},{16,12}... | collective-permute-start | bytes 221192 | tf_op jit(solution)/shard_map/ppermute | solution.py:67
  72.6 2.1 %collective-permute-start.14 = (bf16[1,32,1152]{2,1,0:T(8,128)(2,1)S(1)}, bf16[1,32,1152]{2,1,0:T(8,128)(2,1)S(1)}, u32[]{:S(2)}, u32[]{:S(2)}) collective-permute-start(bf16[1,32,1152]{2,1,0:T(8,128)(2,1)S(1)} %get-tuple-element.5), channel_id=1, source_target_pairs={{0,30},{2,28},{4,26},{6,24},{8,22},{10,20},{12,18},{14,16},{16,14}... | collective-permute-start | bytes 221192 | tf_op jit(solution)/shard_map/ppermute | solution.py:67
  77.9 2.8 %collective-permute-done.14 = bf16[1,32,1152]{2,1,0:T(8,128)(2,1)S(1)} collective-permute-done((bf16[1,32,1152]{2,1,0:T(8,128)(2,1)S(1)}, bf16[1,32,1152]{2,1,0:T(8,128)(2,1)S(1)}, u32[]{:S(2)}, u32[]{:S(2)}) %collective-permute-start.14) | collective-permute-done | bytes 73760 | tf_op jit(solution)/shard_map/ppermute | solution.py:67
  81.3 2.0 %gather_fusion.1 = bf16[16,32,1152]{2,1,0:T(8,128)(2,1)S(1)} fusion(bf16[16,32,1152]{2,1,0:T(8,128)(2,1)} %bitcast.123, s32[1024]{0:T(1024)S(1)} %pad_clamp_fusion.2), kind=kCustom, calls=%fused_computation.1 | custom fusion | bytes 2359360 | tf_op jit(solution)/shard_map/gather | solution.py:68
  83.3 3.3 %copy.39 = bf16[16,32,1152]{1,2,0:T(8,128)(2,1)} copy(bf16[16,32,1152]{2,1,0:T(8,128)(2,1)S(1)} %gather_fusion.1) | data formatting | bytes 2359296 | tf_op jit(solution)/shard_map/gather | solution.py:68
  86.7 19.5 %copy.41 = bf16[16,32,12,2,3,16]{5,2,4,3,1,0:T(8,128)(2,1)} copy(bf16[16,32,12,2,3,16]{1,5,4,3,2,0:T(8,128)(2,1)} %bitcast.120) | data formatting | bytes 2359296 | tf_op jit(solution)/shard_map/reshape;reshape | solution.py:39
  106.2 6.6 %convolution_bitcast_fusion = f32[3,16,32,2,16]{4,0,3,2,1:T(4,128)} fusion(bf16[16,32,12,2,3,16]{5,2,4,3,1,0:T(8,128)(2,1)} %copy.41, bf16[16,32,3,12,3,1]{3,2,4,5,1,0:T(4,128)(2,1)S(1)} %copy.50), kind=kOutput, calls=%fused_computation.11 | convolution fusion | flops 3538944 | bytes 1486848 | tf_op jit(solution)/shard_map/scepk,scpikh->escih/dot_general | solution.py:40
  112.8 1.8 %copy.43 = f32[3,16,32,2,16]{2,1,0,4,3:T(8,128)S(1)} copy(f32[3,16,32,2,16]{4,0,3,2,1:T(4,128)} %convolution_bitcast_fusion) | data formatting | bytes 393216 | tf_op jit(solution)/shard_map/scepk,scpikh->escih/transpose | solution.py:40
  114.9 2.2 %fusion.2 = f32[32,384]{0,1:T(8,128)S(1)} fusion(f32[1536,32]{0,1:T(8,128)S(1)} %reshape.148, s32[1536]{0:T(1024)S(1)} %eq.15), kind=kOutput, calls=%fused_computation.9 | convolution fusion | flops 227082240 | bytes 251904 | tf_op jit(solution)/shard_map/ra,re->ae/dot_general | solution.py:76
  117.9 5.1 %collective-permute-start.15 = (f32[32,32]{0,1:T(8,128)S(1)}, f32[32,32]{0,1:T(8,128)S(1)}, u32[]{:S(2)}, u32[]{:S(2)}) collective-permute-start(f32[32,32]{0,1:T(8,128)S(1)} %bitcast.125), channel_id=1, source_target_pairs={{0,2},{2,4},{4,6},{6,8},{8,10},{10,12},{12,14},{14,16},{16,18},{18... | collective-permute-start | bytes 12296 | tf_op jit(solution)/shard_map/ppermute | solution.py:30
  123.6 1.9 %collective-permute-start.16 = (f32[32,32]{0,1:T(8,128)S(1)}, f32[32,32]{0,1:T(8,128)S(1)}, u32[]{:S(2)}, u32[]{:S(2)}) collective-permute-start(f32[32,32]{0,1:T(8,128)S(1)} %bitcast.124), channel_id=1, source_target_pairs={{2,0},{4,2},{6,4},{8,6},{10,8},{12,10},{14,12},{16,14},{18,16},{20... | collective-permute-start | bytes 12296 | tf_op jit(solution)/shard_map/ppermute | solution.py:31
  126.5 4.5 %collective-permute-done.16 = f32[32,32]{0,1:T(8,128)S(1)} collective-permute-done((f32[32,32]{0,1:T(8,128)S(1)}, f32[32,32]{0,1:T(8,128)S(1)}, u32[]{:S(2)}, u32[]{:S(2)}) %collective-permute-start.16) | collective-permute-done | bytes 4128 | tf_op jit(solution)/shard_map/ppermute | solution.py:31
  (73 shorter events, 25.4 us)
Async XLA Ops:
  0.0 1.5 %copy-start = (bf16[8,2,3,32,256]{4,3,2,1,0:T(8,128)(2,1)S(1)}, bf16[8,2,3,32,256]{4,3,2,1,0:T(8,128)(2,1)}, u32[]{:S(2)}) copy-start(bf16[8,2,3,32,256]{4,3,2,1,0:T(8,128)(2,1)} %param.6) | copy-start | bytes 2359300
  35.7 1.1 copy-start.1
  36.7 7.9 %copy-start.2 = (bf16[1,16,32,108]{3,2,1,0:T(8,128)(2,1)S(1)}, bf16[1,16,32,108]{3,2,1,0:T(8,128)(2,1)}, u32[]{:S(2)}) copy-start(bf16[1,16,32,108]{3,2,1,0:T(8,128)(2,1)} %param.9) | copy-start | bytes 331780
  37.6 10.3 %collective-permute-start = (bf16[1,32,1152]{2,1,0:T(8,128)(2,1)S(1)}, bf16[1,32,1152]{2,1,0:T(8,128)(2,1)S(1)}, u32[]{:S(2)}, u32[]{:S(2)}) collective-permute-start(bf16[1,32,1152]{2,1,0:T(8,128)(2,1)S(1)} %get-tuple-element.19), channel_id=1, source_target_pairs={{0,2},{2,0},{4,6},{6,4},{8,10},{10,8},{12,14},{14,12},{16,18},{18,... | collective-permute-start | bytes 221192 | tf_op jit(solution)/shard_map/ppermute | solution.py:67
  38.2 12.0 %collective-permute-start.1 = (bf16[1,32,1152]{2,1,0:T(8,128)(2,1)}, bf16[1,32,1152]{2,1,0:T(8,128)(2,1)S(1)}, u32[]{:S(2)}, u32[]{:S(2)}) collective-permute-start(bf16[1,32,1152]{2,1,0:T(8,128)(2,1)} %get-tuple-element.18), channel_id=1, source_target_pairs={{0,4},{2,6},{4,0},{6,2},{8,12},{10,14},{12,8},{14,10},{16,20},{18,... | collective-permute-start | bytes 221192 | tf_op jit(solution)/shard_map/ppermute | solution.py:67
  38.2 14.9 %collective-permute-start.2 = (bf16[1,32,1152]{2,1,0:T(8,128)(2,1)}, bf16[1,32,1152]{2,1,0:T(8,128)(2,1)S(1)}, u32[]{:S(2)}, u32[]{:S(2)}) collective-permute-start(bf16[1,32,1152]{2,1,0:T(8,128)(2,1)} %get-tuple-element.17), channel_id=1, source_target_pairs={{0,6},{2,4},{4,2},{6,0},{8,14},{10,12},{12,10},{14,8},{16,22},{18,... | collective-permute-start | bytes 221192 | tf_op jit(solution)/shard_map/ppermute | solution.py:67
  41.2 15.2 %collective-permute-start.3 = (bf16[1,32,1152]{2,1,0:T(8,128)(2,1)}, bf16[1,32,1152]{2,1,0:T(8,128)(2,1)S(1)}, u32[]{:S(2)}, u32[]{:S(2)}) collective-permute-start(bf16[1,32,1152]{2,1,0:T(8,128)(2,1)} %get-tuple-element.16), channel_id=1, source_target_pairs={{0,8},{2,10},{4,12},{6,14},{8,0},{10,2},{12,4},{14,6},{16,24},{18,... | collective-permute-start | bytes 221192 | tf_op jit(solution)/shard_map/ppermute | solution.py:67
  42.7 14.6 %collective-permute-start.4 = (bf16[1,32,1152]{2,1,0:T(8,128)(2,1)}, bf16[1,32,1152]{2,1,0:T(8,128)(2,1)S(1)}, u32[]{:S(2)}, u32[]{:S(2)}) collective-permute-start(bf16[1,32,1152]{2,1,0:T(8,128)(2,1)} %get-tuple-element.15), channel_id=1, source_target_pairs={{0,10},{2,8},{4,14},{6,12},{8,2},{10,0},{12,6},{14,4},{16,26},{18,... | collective-permute-start | bytes 221192 | tf_op jit(solution)/shard_map/ppermute | solution.py:67
  44.7 2.1 %copy-start.7 = (s32[1,2,32]{2,1,0:T(2,128)S(1)}, s32[1,2,32]{2,1,0:T(2,128)}, u32[]{:S(2)}) copy-start(s32[1,2,32]{2,1,0:T(2,128)} %param.11) | copy-start | bytes 772
  45.1 1.6 %copy-start.4 = (s32[3,1,16,32]{3,2,1,0:T(8,128)S(1)}, s32[3,1,16,32]{3,2,1,0:T(8,128)}, u32[]{:S(2)}) copy-start(s32[3,1,16,32]{3,2,1,0:T(8,128)} %param.10) | copy-start | bytes 18436
  45.1 23.4 %copy-start.3 = (bf16[1,32,1152]{2,1,0:T(8,128)(2,1)S(1)}, bf16[1,32,1152]{2,1,0:T(8,128)(2,1)}, u32[]{:S(2)}) copy-start(bf16[1,32,1152]{2,1,0:T(8,128)(2,1)} %get-tuple-element.6) | copy-start | bytes 221188
  46.8 34.5 %copy-start.6 = (s32[32]{0:T(128)}, s32[32]{0:T(128)S(1)}, u32[]{:S(2)}) copy-start(s32[32]{0:T(128)S(1)} %get-tuple-element.21) | copy-start | bytes 388
  48.0 12.5 %collective-permute-start.5 = (bf16[1,32,1152]{2,1,0:T(8,128)(2,1)S(1)}, bf16[1,32,1152]{2,1,0:T(8,128)(2,1)S(1)}, u32[]{:S(2)}, u32[]{:S(2)}) collective-permute-start(bf16[1,32,1152]{2,1,0:T(8,128)(2,1)S(1)} %get-tuple-element.14), channel_id=1, source_target_pairs={{0,12},{2,14},{4,8},{6,10},{8,4},{10,6},{12,0},{14,2},{16,28},{18,... | collective-permute-start | bytes 221192 | tf_op jit(solution)/shard_map/ppermute | solution.py:67
  50.2 13.2 %collective-permute-start.6 = (bf16[1,32,1152]{2,1,0:T(8,128)(2,1)}, bf16[1,32,1152]{2,1,0:T(8,128)(2,1)S(1)}, u32[]{:S(2)}, u32[]{:S(2)}) collective-permute-start(bf16[1,32,1152]{2,1,0:T(8,128)(2,1)} %get-tuple-element.13), channel_id=1, source_target_pairs={{0,14},{2,12},{4,10},{6,8},{8,6},{10,4},{12,2},{14,0},{16,30},{18,... | collective-permute-start | bytes 221192 | tf_op jit(solution)/shard_map/ppermute | solution.py:67
  53.2 14.4 %collective-permute-start.7 = (bf16[1,32,1152]{2,1,0:T(8,128)(2,1)}, bf16[1,32,1152]{2,1,0:T(8,128)(2,1)S(1)}, u32[]{:S(2)}, u32[]{:S(2)}) collective-permute-start(bf16[1,32,1152]{2,1,0:T(8,128)(2,1)} %get-tuple-element.12), channel_id=1, source_target_pairs={{0,16},{2,18},{4,20},{6,22},{8,24},{10,26},{12,28},{14,30},{16,0},... | collective-permute-start | bytes 221192 | tf_op jit(solution)/shard_map/ppermute | solution.py:67
  56.4 12.1 %collective-permute-start.8 = (bf16[1,32,1152]{2,1,0:T(8,128)(2,1)}, bf16[1,32,1152]{2,1,0:T(8,128)(2,1)S(1)}, u32[]{:S(2)}, u32[]{:S(2)}) collective-permute-start(bf16[1,32,1152]{2,1,0:T(8,128)(2,1)} %get-tuple-element.11), channel_id=1, source_target_pairs={{0,18},{2,16},{4,22},{6,20},{8,26},{10,24},{12,30},{14,28},{16,2},... | collective-permute-start | bytes 221192 | tf_op jit(solution)/shard_map/ppermute | solution.py:67
  57.3 15.3 %collective-permute-start.9 = (bf16[1,32,1152]{2,1,0:T(8,128)(2,1)}, bf16[1,32,1152]{2,1,0:T(8,128)(2,1)S(1)}, u32[]{:S(2)}, u32[]{:S(2)}) collective-permute-start(bf16[1,32,1152]{2,1,0:T(8,128)(2,1)} %get-tuple-element.10), channel_id=1, source_target_pairs={{0,20},{2,22},{4,16},{6,18},{8,28},{10,30},{12,24},{14,26},{16,4},... | collective-permute-start | bytes 221192 | tf_op jit(solution)/shard_map/ppermute | solution.py:67
  60.5 14.9 %collective-permute-start.10 = (bf16[1,32,1152]{2,1,0:T(8,128)(2,1)}, bf16[1,32,1152]{2,1,0:T(8,128)(2,1)S(1)}, u32[]{:S(2)}, u32[]{:S(2)}) collective-permute-start(bf16[1,32,1152]{2,1,0:T(8,128)(2,1)} %get-tuple-element.9), channel_id=1, source_target_pairs={{0,22},{2,20},{4,18},{6,16},{8,30},{10,28},{12,26},{14,24},{16,6},... | collective-permute-start | bytes 221192 | tf_op jit(solution)/shard_map/ppermute | solution.py:67
  63.4 12.6 %collective-permute-start.11 = (bf16[1,32,1152]{2,1,0:T(8,128)(2,1)}, bf16[1,32,1152]{2,1,0:T(8,128)(2,1)S(1)}, u32[]{:S(2)}, u32[]{:S(2)}) collective-permute-start(bf16[1,32,1152]{2,1,0:T(8,128)(2,1)} %get-tuple-element.8), channel_id=1, source_target_pairs={{0,24},{2,26},{4,28},{6,30},{8,16},{10,18},{12,20},{14,22},{16,8},... | collective-permute-start | bytes 221192 | tf_op jit(solution)/shard_map/ppermute | solution.py:67
  67.6 9.0 %collective-permute-start.12 = (bf16[1,32,1152]{2,1,0:T(8,128)(2,1)}, bf16[1,32,1152]{2,1,0:T(8,128)(2,1)S(1)}, u32[]{:S(2)}, u32[]{:S(2)}) collective-permute-start(bf16[1,32,1152]{2,1,0:T(8,128)(2,1)} %get-tuple-element.7), channel_id=1, source_target_pairs={{0,26},{2,24},{4,30},{6,28},{8,18},{10,16},{12,22},{14,20},{16,10}... | collective-permute-start | bytes 221192 | tf_op jit(solution)/shard_map/ppermute | solution.py:67
  68.4 8.8 %collective-permute-start.13 = (bf16[1,32,1152]{2,1,0:T(8,128)(2,1)S(1)}, bf16[1,32,1152]{2,1,0:T(8,128)(2,1)S(1)}, u32[]{:S(2)}, u32[]{:S(2)}) collective-permute-start(bf16[1,32,1152]{2,1,0:T(8,128)(2,1)S(1)} %copy-done.3), channel_id=1, source_target_pairs={{0,28},{2,30},{4,24},{6,26},{8,20},{10,22},{12,16},{14,18},{16,12}... | collective-permute-start | bytes 221192 | tf_op jit(solution)/shard_map/ppermute | solution.py:67
  72.6 8.1 %collective-permute-start.14 = (bf16[1,32,1152]{2,1,0:T(8,128)(2,1)S(1)}, bf16[1,32,1152]{2,1,0:T(8,128)(2,1)S(1)}, u32[]{:S(2)}, u32[]{:S(2)}) collective-permute-start(bf16[1,32,1152]{2,1,0:T(8,128)(2,1)S(1)} %get-tuple-element.5), channel_id=1, source_target_pairs={{0,30},{2,28},{4,26},{6,24},{8,22},{10,20},{12,18},{14,16},{16,14}... | collective-permute-start | bytes 221192 | tf_op jit(solution)/shard_map/ppermute | solution.py:67
  117.9 7.6 %collective-permute-start.15 = (f32[32,32]{0,1:T(8,128)S(1)}, f32[32,32]{0,1:T(8,128)S(1)}, u32[]{:S(2)}, u32[]{:S(2)}) collective-permute-start(f32[32,32]{0,1:T(8,128)S(1)} %bitcast.125), channel_id=1, source_target_pairs={{0,2},{2,4},{4,6},{6,8},{8,10},{10,12},{12,14},{14,16},{16,18},{18... | collective-permute-start | bytes 12296 | tf_op jit(solution)/shard_map/ppermute | solution.py:30
  123.6 7.4 %collective-permute-start.16 = (f32[32,32]{0,1:T(8,128)S(1)}, f32[32,32]{0,1:T(8,128)S(1)}, u32[]{:S(2)}, u32[]{:S(2)}) collective-permute-start(f32[32,32]{0,1:T(8,128)S(1)} %bitcast.124), channel_id=1, source_target_pairs={{2,0},{4,2},{6,4},{8,6},{10,8},{12,10},{14,12},{16,14},{18,16},{20... | collective-permute-start | bytes 12296 | tf_op jit(solution)/shard_map/ppermute | solution.py:31
  (1 other events, 0.6 us)
